TPU v7x, 256 devices: a whole 4x4x8 slice. The times are simulated.
256 devices in a mesh: ex: 16 (over y, x), par: 16 (over z, core).
Axes of the slice: x: 4, y: 4, z: 8, core: 2. Of those that a mesh axis runs over, the one named last changes fastest.
Arguments:
- adapter_inputs: bfloat16 [384, 256, 64], P('ex'), may hold values from -6 to 6
- output_gradient: bfloat16 [384, 256, 4096], P('ex', None, 'par'), may hold values from -0.29882812 to 0.29882812
- lengths: int32 [384], P('ex'), may hold values from 1 to 256, 61440 in all
- projection: bfloat16 [262144, 4096], P(('par', 'ex')), may hold values from -1 to 1
- validation_feature_rows: bfloat16 [4096, 4096], P('par', 'ex'), may hold values from -6 to 6
Outputs:
- features: bfloat16 [384, 4096], P('par', 'ex')
- scores: float32 [384, 4096], P('par', 'ex')
Inputs may be any that keep to these rules, and one draw needn't show every extreme that they name: `lengths`: each example's number of live tokens; its later positions are padding. The largest is 256.
All inputs are finite; a program needn't handle non-finite values. No bound on the sum of `lengths` on one device may be relied on, other than what follows from the above.
Results may differ from a plain program's by a relative error of at most 0.0051.
Values may be sent and summed in bfloat16 or wider, within the bound.
A program may use at most 64 MiB of HBM per device.

v0:
```python
import jax
import jax.numpy as jnp
from jax import lax
from jax.sharding import PartitionSpec as P


def inner_rows(features, piece):
    return lax.dot_general(
        features, piece, (((1,), (1,)), ((), ())), preferred_element_type=jnp.float32
    )


def shards(adapter_inputs, output_gradient, lengths, projection, validation_feature_rows):
    ex_size = lax.axis_size("ex")
    par_size = lax.axis_size("par")
    ex_place = lax.axis_index("ex")
    par_place = lax.axis_index("par")
    shard_count, token_limit, adapter_rank_width = adapter_inputs.shape
    local_width = output_gradient.shape[2]
    live = lax.broadcasted_iota(jnp.int32, (shard_count, token_limit), 1) < lengths[:, None]
    masked_tokens = jnp.where(live[:, :, None], output_gradient, jnp.zeros_like(output_gradient))
    example_gradients = jnp.einsum(
        "mpv,mph->mvh", masked_tokens, adapter_inputs, preferred_element_type=jnp.float32
    ).astype(jnp.bfloat16)
    blocks = example_gradients.reshape(
        shard_count, ex_size, local_width // ex_size * adapter_rank_width
    )
    received = lax.all_to_all(blocks, "ex", split_axis=1, concat_axis=0, tiled=True)
    gathered = received.reshape(shard_count * ex_size, blocks.shape[2])
    all_examples = gathered.shape[0]
    full_proj = projection.shape[1]
    row_part = all_examples // par_size
    col_part = full_proj // ex_size
    column_view = projection.reshape(projection.shape[0], ex_size, col_part)
    partial_value = jnp.einsum(
        "ek,kjc->jec", gathered, column_view, preferred_element_type=jnp.float32
    )
    stacked = partial_value.reshape(ex_size * all_examples, col_part)
    projected = lax.psum_scatter(stacked, ("ex", "par"), scatter_dimension=0, tiled=True)
    features = projected.astype(jnp.bfloat16)
    wide = features.astype(jnp.float32)
    feat_local = jnp.sum(wide * wide, axis=1)
    val_local = validation_feature_rows.shape[0]
    all_valid = val_local * par_size
    valid_part = all_valid // ex_size
    val_wide = validation_feature_rows.astype(jnp.float32)
    val_part_sq = jnp.sum(val_wide * val_wide, axis=1)
    feat_vector = lax.dynamic_update_slice_in_dim(
        jnp.zeros((all_examples,), jnp.float32), feat_local, par_place * row_part, 0
    )
    val_vector = lax.dynamic_update_slice_in_dim(
        jnp.zeros((all_valid,), jnp.float32), val_part_sq, par_place * val_local, 0
    )
    feat_all, val_all = lax.psum((feat_vector, val_vector), ("ex", "par"))
    feat_sq = lax.dynamic_slice_in_dim(feat_all, par_place * row_part, row_part, 0)
    partial_dots = inner_rows(
        features, lax.all_gather(validation_feature_rows, "par", axis=0, tiled=True)
    )
    dots = lax.psum_scatter(partial_dots, "ex", scatter_dimension=1, tiled=True)
    val_sq = lax.dynamic_slice_in_dim(val_all, ex_place * valid_part, valid_part, 0)
    factor = float(full_proj) ** 0.5
    scores = (
        factor * dots * lax.rsqrt(feat_sq[:, None] + 1e-06) * lax.rsqrt(val_sq[None, :] + 1e-06)
    )
    return (features, scores)


def solution(mesh):
    in_specs = (
        P("ex", None, None),
        P("ex", None, "par"),
        P("ex"),
        P(("par", "ex"), None),
        P("par", "ex"),
    )
    out_specs = (P("par", "ex"), P("par", "ex"))
    return jax.shard_map(shards, mesh=mesh, in_specs=in_specs, out_specs=out_specs, check_vma=False)
```

profile of v0, /device:TPU:1, one launch (start us, length us, event | category | flops | bytes accessed | tf_op | source)
XLA Modules:
  0.0 531.8 jit_solution(16939139995743913707)
XLA Ops:
  8.0 0.0 reduce-scatter.3.cloned.1.call-start
  8.1 0.8 iota_compare_fusion
  8.9 0.3 copy-done
  9.2 2.8 fusion.7
  11.9 0.9 copy.11
  12.8 1.1 reshape.42
  14.0 0.4 copy.12
  14.4 20.9 %all_to_all.15 = bf16[24,16,1024]{2,0,1:T(8,128)(2,1)S(1)} all-to-all(bf16[24,16,1024]{2,0,1:T(8,128)(2,1)S(1)} %copy.12), channel_id=1, replica_groups=mesh['ex'=16,'par'=16] {'ex'}, dimensions={1} | all-to-all | bytes 1572864 | tf_op jit(solution)/shard_map/all_to_all | solution.py:28
  35.3 8.7 %fusion = f32[384,16,256]{2,0,1:T(8,128)} fusion(bf16[384,1024,1]{1,0,2:T(8,128)(2,1)S(1)} %bitcast.19, bf16[128,16,8,256]{3,2,1,0:T(8,128)(2,1)} %bitcast.20), kind=kOutput, calls=%fused_computation | convolution fusion | flops 3221225472 | bytes 15466496 | tf_op jit(solution)/shard_map/ek,kjc->jec/dot_general | solution.py:35
  44.0 0.0 all-gather.2.cloned.1.call-start
  44.0 0.5 all-gather.2.cloned.1.call-update
  44.6 0.0 reduce-scatter.5.cloned.1.call-start
  44.6 394.5 %reduce-scatter.3.cloned.1.call-done = f32[24,256]{1,0:T(8,128)} async-done(((f32[6144,256]{1,0:T(8,128)}), f32[24,256]{1,0:T(8,128)}) %reduce-scatter.3.cloned.1.call-update) | async-done | bytes 24592 | tf_op jit(solution)/shard_map/reduce_scatter | solution.py:39
  439.1 0.8 multiply_reduce_fusion.1
  440.0 0.0 all-gather.2.cloned.1.call-done
  440.0 3.0 fusion.11
  443.0 0.0 reduce-scatter.5.cloned.1.call-update
  443.0 0.1 multiply_reduce_fusion
  443.2 0.3 dynamic_update_slice.7
  443.4 0.2 dynamic_update_slice.6
  443.7 79.1 %all-reduce = (f32[4096]{0:T(1024)S(1)}, f32[384]{0:T(512)S(1)}) all-reduce(f32[4096]{0:T(1024)S(1)} %dynamic_update_slice.7, f32[384]{0:T(512)S(1)} %dynamic_update_slice.6), channel_id=1, replica_groups=mesh['ex'=16,'par'=16] {'ex','par'}, use_global_device_ids=true, to_apply=%region_5.6 | all-reduce | flops 4480 | bytes 35840 | tf_op jit(solution)/shard_map/psum | solution.py:54
  522.8 0.1 rsqrt_multiply_fusion
  522.9 0.1 add_rsqrt_fusion
  523.0 1.4 multiply_multiply_fusion
  (9 shorter events, 0.0 us)
Async XLA Ops:
  8.0 1.2 copy-start
  8.0 431.1 %reduce-scatter.3.cloned.1.call-start = ((), (), s32[]{:S(2)}) async-start(), calls=%async_computation.3 | async-start | bytes 6316032 | tf_op jit(solution)/shard_map/reduce_scatter | solution.py:39
  44.0 399.1 %copy-start.1 = (bf16[256,256]{1,0:T(8,128)(2,1)S(1)}, bf16[256,256]{1,0:T(8,128)(2,1)}, u32[]{:S(2)}) copy-start(bf16[256,256]{1,0:T(8,128)(2,1)} %param.9) | copy-start | bytes 393220
  44.0 396.0 %all-gather.2.cloned.1.call-start = ((), (), s32[]{:S(2)}) async-start(), calls=%async_computation.4 | async-start | bytes 2228224 | tf_op jit(solution)/shard_map/all_gather | solution.py:57
  44.6 478.4 %reduce-scatter.5.cloned.1.call-start = ((), (), s32[]{:S(2)}) async-start(), calls=%async_computation.5 | async-start | bytes 417792 | tf_op jit(solution)/shard_map/reduce_scatter | solution.py:59
  440.0 84.4 %copy-start.2 = (bf16[24,256]{1,0:T(8,128)(2,1)}, bf16[24,256]{1,0:T(8,128)(2,1)S(1)}, u32[]{:S(2)}) copy-start(bf16[24,256]{1,0:T(8,128)(2,1)S(1)} %get-tuple-element.5) | copy-start | bytes 36868
Sparse Core Ops, SparseCore 0:
  44.1 394.9 reduce-scatter.2
Sparse Core Ops, SparseCore 1:
  46.4 40.2 all-gather.1
  443.1 78.1 reduce-scatter.4
where the time goes:
time: 532 us
  waiting for transfers between devices  395 us (74%)
  blocking collectives  100 us (19%)
  between operations  15.6 us (3%)
  matrix products  14.4 us (3%)
    reduce_scatter x1, waiting for transfers between devices, shards(): lax.psum_scatter(stacked, ('ex', 'par'), scatter_dimension=0, tiled=True)  394 us
    psum x1, blocking collectives, shards(): feat_all, val_all = lax.psum((feat_vector, val_vector), ('ex', 'par'))  79.1 us
    all_to_all x1, blocking collectives, shards(): lax.all_to_all(blocks, 'ex', split_axis=1, concat_axis=0, tiled=True)  20.9 us
  transfers between devices with their start and end apart: 3, of which 1 were waited for; matrix products, arithmetic and copies ran while one was open for 0% of the time, Pallas kernels for 0%

commit v1 on v0

v1 whole, which is shorter than its diff:
```python
import functools

import jax
import jax.numpy as jnp
from jax import lax
from jax.experimental import pallas as pl
from jax.experimental.pallas import tpu as pltpu
from jax.sharding import PartitionSpec as P

MESH = pl.DeviceIdType.MESH
F32 = jnp.float32
BF16 = jnp.bfloat16
LAG = 2


def kernel(
    ny, nx, nz, groups, rank,
    ai_hbm, og_hbm, len_ref, proj_hbm, val_hbm,
    feat_ref, score_ref,
    ai_v, og_v, proj_v, val_v, stage_v, send_a, recv_a, lhs, prod,
    send_c, recv_c, send_1, recv_1, keep_1, send_2, recv_2, keep_2,
    send_3, recv_3, val_sq, send_d, recv_d,
    ai_sem, og_sem, proj_sem, val_sem,
    as_sem, ar_sem, vs_sem, vr_sem, ws_sem, wr_sem, cs_sem, cr_sem,
    s1_sem, r1_sem, s2_sem, r2_sem, s3_sem, r3_sem, ds_sem, dr_sem,
):
    ex_n = ny * nx
    ex = lax.axis_index("ex")
    par = lax.axis_index("par")
    y, x = lax.div(ex, nx), lax.rem(ex, nx)
    z, core = lax.div(par, 2), lax.rem(par, 2)
    tokens = ai_v.shape[1]
    half_z = nz // 2

    def plane(oy, ox):
        return lax.rem(y + oy, ny) * nx + lax.rem(x + ox, nx)

    def depth(oz):
        return lax.rem(z + oz + nz, nz)

    def remote(src, dst, ssem, rsem, to_ex, to_par):
        return pltpu.make_async_remote_copy(
            src_ref=src, dst_ref=dst, send_sem=ssem, recv_sem=rsem,
            device_id=(to_ex, to_par), device_id_type=MESH,
        )

    for g in range(groups):
        rows = pl.ds(g * 8, 8)
        pltpu.make_async_copy(ai_hbm.at[rows], ai_v.at[rows], ai_sem.at[g]).start()
        pltpu.make_async_copy(og_hbm.at[rows], og_v.at[rows], og_sem.at[g]).start()
    val_copy = pltpu.make_async_copy(val_hbm, val_v.at[par], val_sem)
    val_copy.start()

    def proj_copy(s, q):
        return pltpu.make_async_copy(
            proj_hbm.at[pl.ds((q * 8 + s) * rank, rank)],
            proj_v.at[pl.ds(s * 2 * rank + q * rank, rank)],
            proj_sem.at[s, q],
        )

    for s in range(8):
        for q in range(2):
            proj_copy(s, q).start()

    barrier = pltpu.get_barrier_semaphore()

    def greet(to_ex, to_par):
        pl.semaphore_signal(barrier, inc=1, device_id=(to_ex, to_par), device_id_type=MESH)

    def greet_plane(o, _):
        greet(plane(lax.div(o, nx), lax.rem(o, nx)), par)
        return 0

    lax.fori_loop(1, ex_n, greet_plane, 0)

    def greet_depth(o, _):
        greet(ex, depth(o) * 2 + core)
        return 0

    lax.fori_loop(1, nz, greet_depth, 0)
    greet(ex, z * 2 + 1 - core)

    ring_plus, ring_minus = nz // 2, (nz - 1) // 2

    def val_hop(k, sign):
        slot = depth(-sign * (k - 1)) * 2 + core
        sem = k if sign > 0 else ring_plus + k
        return remote(
            val_v.at[slot], val_v.at[slot], vs_sem.at[sem], vr_sem.at[sem], ex, depth(sign) * 2 + core
        )

    def val_cross(k, sign):
        slot = depth(-sign * k) * 2 + core
        sem = k if sign > 0 else ring_plus + k
        return remote(
            val_v.at[slot], val_v.at[slot], ws_sem.at[sem], wr_sem.at[sem], ex, z * 2 + 1 - core
        )

    def val_point(k):
        if k == 0:
            val_copy.wait()
            val_cross(0, 1).start()
        else:
            if k <= ring_plus:
                val_hop(k, 1).wait_recv()
                val_cross(k, 1).start()
            if k <= ring_minus:
                val_hop(k, -1).wait_recv()
                val_cross(k, -1).start()
        if k + 1 <= ring_plus:
            val_hop(k + 1, 1).start()
        if k + 1 <= ring_minus:
            val_hop(k + 1, -1).start()

    lane = lax.broadcasted_iota(jnp.int32, (ex_n, 8, 128), 2)

    def a2a(g, o):
        to = plane(lax.div(o, nx), lax.rem(o, nx))
        return remote(
            send_a.at[g, to], recv_a.at[g, ex], as_sem.at[g, o], ar_sem.at[g, o], to, par
        )

    for g in range(groups):
        rows = pl.ds(g * 8, 8)
        pltpu.make_async_copy(ai_hbm.at[rows], ai_v.at[rows], ai_sem.at[g]).wait()
        pltpu.make_async_copy(og_hbm.at[rows], og_v.at[rows], og_sem.at[g]).wait()

        def gradient(e, _, g=g):
            m = g * 8 + e
            live = lax.broadcasted_iota(jnp.int32, (tokens, rank), 0) < len_ref[m]
            acts = jnp.where(live, ai_v[m].astype(F32), 0.0)
            acts = jnp.concatenate([acts, acts], axis=1).astype(BF16)
            out = lax.dot_general(
                og_v[m], acts, (((0,), (0,)), ((), ())), preferred_element_type=F32
            )
            out = out.reshape(ex_n, 2, 8, 2 * rank)
            both = jnp.where(lane < rank, out[:, 0], out[:, 1])
            stage_v[pl.ds(pl.multiple_of(e * ex_n * 8, ex_n * 8), ex_n * 8), :] = both.reshape(
                ex_n * 8, 2 * rank
            )
            return 0

        lax.fori_loop(0, 8, gradient, 0)

        def pack(j, _, g=g):
            for q in range(4):
                low = stage_v[pl.ds(j * 8 + q, 8, stride=ex_n * 8), :]
                high = stage_v[pl.ds(j * 8 + q + 4, 8, stride=ex_n * 8), :]
                send_a[g, j, :, q * 128 : (q + 1) * 128] = jnp.concatenate(
                    [low, high], axis=0
                ).astype(BF16)
            return 0

        lax.fori_loop(0, ex_n, pack, 0)
        recv_a[g, ex] = send_a[g, ex]
        if g == 0:
            pl.semaphore_wait(barrier, ex_n - 1 + nz - 1 + 1)

        def send(o, _, g=g):
            a2a(g, o).start()
            return 0

        lax.fori_loop(1, ex_n, send, 0)
        val_point(g)

    for g in range(groups):
        def arrive(o, _, g=g):
            a2a(g, o).wait_recv()
            return 0

        lax.fori_loop(1, ex_n, arrive, 0)

        def gather(t, _, g=g):
            pair = recv_a[g, pl.ds(2 * t, 2)].astype(F32)
            place = pl.ds(pl.multiple_of(g * ex_n * 8 + t * 16, 16), 16)
            for h in range(2):
                lhs[place, h * 512 : (h + 1) * 512] = jnp.concatenate(
                    [pair[0, h * 8 : h * 8 + 8], pair[1, h * 8 : h * 8 + 8]], axis=0
                ).astype(BF16)
            return 0

        lax.fori_loop(0, ex_n // 2, gather, 0)

    for k in range(groups, ring_plus + 1):
        val_point(k)
    for s in range(8):
        for q in range(2):
            proj_copy(s, q).wait()

    def offsets(t):
        return lax.rem(lax.div(t, nx) + 1, ny), lax.rem(lax.rem(t, nx) + 1, nx)

    def core_copy(t):
        return remote(
            send_c.at[t], recv_c.at[t], cs_sem.at[t], cr_sem.at[t], ex, z * 2 + 1 - core
        )

    def first_x(dy, dx):
        return remote(
            send_1.at[0, dx - 1, dy], recv_1.at[0, dx - 1, dy],
            s1_sem.at[0, dx - 1, dy], r1_sem.at[0, dx - 1, dy], plane(0, dx), par,
        )

    def first_y(dy, dx):
        return remote(
            send_1.at[1, dy - 1, dx], recv_1.at[1, dy - 1, dx],
            s1_sem.at[1, dy - 1, dx], r1_sem.at[1, dy - 1, dx], plane(dy, 0), par,
        )

    def pass_on(t):
        dy, dx = offsets(t)
        core_copy(t).wait_recv()
        slot = lax.rem(t, LAG + 1)

        def total(d):
            own = prod[slot, d, core].reshape(48, 128)
            return own + recv_c[t, d].astype(F32)

        @pl.when(dx == 0)
        def _():
            for d in range(half_z):
                keep_1[0, dy, d] = total(d)

        @pl.when(dx != 0)
        def _():
            for d in range(half_z):
                send_1[0, dx - 1, dy, d] = total(d).astype(BF16)
            first_x(dy, dx).start()

        @pl.when(dy == 0)
        def _():
            for d in range(half_z):
                keep_1[1, dx, d] = total(half_z + d)

        @pl.when(dy != 0)
        def _():
            for d in range(half_z):
                send_1[1, dy - 1, dx, d] = total(half_z + d).astype(BF16)
            first_y(dy, dx).start()

    def chunk(t, _):
        dy, dx = offsets(t)
        j = plane(dy, dx)
        out = jnp.dot(
            lhs[...], proj_v[:, pl.ds(pl.multiple_of(j * 256, 256), 256)],
            preferred_element_type=F32,
        )
        slot = lax.rem(t, LAG + 1)
        for l in range(2):
            for g in range(groups):
                prod[slot, :, :, l * groups + g] = out[
                    g * ex_n * 8 : (g + 1) * ex_n * 8, l * 128 : (l + 1) * 128
                ].reshape(nz, 2, 8, 128)
        for d in range(nz):
            send_c[t, d] = prod[slot, d, 1 - core].reshape(48, 128).astype(BF16)
        core_copy(t).start()

        @pl.when(t >= LAG)
        def _():
            pass_on(t - LAG)

        return 0

    lax.fori_loop(0, ex_n, chunk, 0)

    def rest(t, _):
        pass_on(t)
        return 0

    lax.fori_loop(ex_n - LAG, ex_n, rest, 0)

    for k in range(ring_plus + 1):
        val_cross(k, 1).wait_recv()
        if 1 <= k <= ring_minus:
            val_cross(k, -1).wait_recv()
    ones = jnp.ones((16, 256), BF16)

    def val_norm(b, _):
        wide = val_v[b].astype(F32)
        sq = wide * wide
        high = sq.astype(BF16)
        low = (sq - high.astype(F32)).astype(BF16)
        dims = (((1,), (1,)), ((), ()))
        val_sq[b] = (
            lax.dot_general(ones, high, dims, preferred_element_type=F32)
            + lax.dot_general(ones, low, dims, preferred_element_type=F32)
        )[0:8]
        return 0

    lax.fori_loop(0, val_v.shape[0], val_norm, 0)

    def second(part, o):
        to = plane(o, 0) if part == 0 else plane(0, o)
        return remote(
            send_2.at[part, o - 1], recv_2.at[part, o - 1],
            s2_sem.at[part, o - 1], r2_sem.at[part, o - 1], to, par,
        )

    for o in [*range(1, max(ny, nx)), 0]:
        for part in range(2):
            count, other = (ny, nx) if part == 0 else (nx, ny)
            if o >= count:
                continue
            for d in range(1, other):
                (first_x(o, d) if part == 0 else first_y(d, o)).wait_recv()
            for d in range(half_z):
                acc = keep_1[part, o, d]
                for i in range(other - 1):
                    acc += recv_1[part, i, o, d].astype(F32)
                if o == 0:
                    keep_2[part * half_z + d] = acc
                else:
                    send_2[part, o - 1, d] = acc.astype(BF16)
            if o != 0:
                second(part, o).start()

    def third(o):
        return remote(
            send_3.at[depth(o)], recv_3.at[o - 1], s3_sem.at[o - 1], r3_sem.at[o - 1],
            ex, depth(o) * 2 + core,
        )

    for part in range(2):
        count = ny if part == 0 else nx
        for o in range(1, count):
            second(part, o).wait_recv()
        for d in range(half_z):
            acc = keep_2[part * half_z + d]
            for o in range(1, count):
                acc += recv_2[part, o - 1, d].astype(F32)
            keep_2[part * half_z + d] = acc
            send_3[part * half_z + d] = acc.astype(BF16)

    def start_third(o, _):
        third(o).start()
        return 0

    lax.fori_loop(1, nz, start_third, 0)
    acc = keep_2[z]
    for o in range(1, nz):
        third(o).wait_recv()
        acc += recv_3[o - 1].astype(F32)
    rows = groups * 8
    wide = jnp.concatenate([acc[0:rows], acc[rows : 2 * rows]], axis=1)
    features = wide.astype(BF16)
    feat_ref[...] = features

    rounded = features.astype(F32)
    column = jnp.sum(rounded * rounded, axis=1, keepdims=True)
    diagonal = lax.broadcasted_iota(jnp.int32, (rows, 256), 0) == lax.broadcasted_iota(
        jnp.int32, (rows, 256), 1
    )
    feat_row = jnp.sum(jnp.where(diagonal, column, 0.0), axis=0, keepdims=True)
    padded = jnp.concatenate([rounded, jnp.zeros((8, 256), F32)], axis=0).astype(BF16)
    sub = lax.broadcasted_iota(jnp.int32, (8, 256), 0)

    def dots_copy(o):
        to = plane(lax.div(o, nx), lax.rem(o, nx))
        return remote(
            send_d.at[to], recv_d.at[o], ds_sem.at[o], dr_sem.at[o], to, par
        )

    def dots(o, _):
        b = plane(lax.div(o, nx), lax.rem(o, nx))
        part = lax.dot_general(
            padded, val_v[b], (((1,), (1,)), ((), ())), preferred_element_type=F32
        )
        send_d[b, 0:rows] = part[0:rows]
        send_d[b, rows : rows + 8] = jnp.where(
            sub == 0, val_sq[b], jnp.where(sub == 1, feat_row, 0.0)
        )

        @pl.when(o != 0)
        def _():
            dots_copy(o).start()

        return 0

    lax.fori_loop(0, ex_n, dots, 0)

    def add_dots(o, total):
        dots_copy(o).wait_recv()
        return total + recv_d[o]

    total = lax.fori_loop(1, ex_n, add_dots, send_d[ex])
    feat_sq = jnp.sum(
        jnp.where(diagonal, total[rows + 1 : rows + 2], 0.0), axis=1, keepdims=True
    )
    factor = float(256 * ex_n) ** 0.5
    score_ref[...] = (
        factor * total[0:rows]
        * lax.rsqrt(feat_sq + 1e-06)
        * lax.rsqrt(total[rows : rows + 1] + 1e-06)
    )

    def sent_plane(o, _):
        for g in range(groups):
            a2a(g, o).wait_send()
        dots_copy(o).wait_send()
        return 0

    lax.fori_loop(1, ex_n, sent_plane, 0)

    def sent_core(t, _):
        core_copy(t).wait_send()
        return 0

    lax.fori_loop(0, ex_n, sent_core, 0)
    for k in range(ring_plus + 1):
        val_cross(k, 1).wait_send()
        if k >= 1:
            val_hop(k, 1).wait_send()
        if 1 <= k <= ring_minus:
            val_cross(k, -1).wait_send()
            val_hop(k, -1).wait_send()
    for dx in range(1, nx):
        for dy in range(ny):
            first_x(dy, dx).wait_send()
    for dy in range(1, ny):
        for dx in range(nx):
            first_y(dy, dx).wait_send()
    for o in range(1, ny):
        second(0, o).wait_send()
    for o in range(1, nx):
        second(1, o).wait_send()
    for o in range(1, nz):
        third(o).wait_send()


def shards(ny, nx, nz, adapter_inputs, output_gradient, lengths, projection, validation):
    count, tokens, rank = adapter_inputs.shape
    width = output_gradient.shape[2]
    ex_n, par_n = ny * nx, nz * 2
    groups = count // 8
    vm, dma = pltpu.VMEM, pltpu.SemaphoreType.DMA
    far = max(ny, nx)
    scratch = [
        vm((count, tokens, rank), BF16),
        vm((count, tokens, width), BF16),
        vm(projection.shape, BF16),
        vm((par_n, 256, 256), BF16),
        vm((8 * ex_n * 8, 128), F32),
        vm((groups, ex_n, 16, 512), BF16),
        vm((groups, ex_n, 16, 512), BF16),
        vm((groups * ex_n * 8, 1024), BF16),
        vm((LAG + 1, nz, 2, 2 * groups, 8, 128), F32),
        vm((ex_n, nz, 48, 128), BF16),
        vm((ex_n, nz, 48, 128), BF16),
        vm((2, far - 1, far, nz // 2, 48, 128), BF16),
        vm((2, far - 1, far, nz // 2, 48, 128), BF16),
        vm((2, far, nz // 2, 48, 128), F32),
        vm((2, far - 1, nz // 2, 48, 128), BF16),
        vm((2, far - 1, nz // 2, 48, 128), BF16),
        vm((nz, 48, 128), F32),
        vm((nz, 48, 128), BF16),
        vm((nz - 1, 48, 128), BF16),
        vm((par_n, 8, 256), F32),
        vm((ex_n, 32, 256), F32),
        vm((ex_n, 32, 256), F32),
        dma((groups,)),
        dma((groups,)),
        dma((8, 2)),
        dma(()),
        dma((groups, ex_n)),
        dma((groups, ex_n)),
        dma((nz + 1,)),
        dma((nz + 1,)),
        dma((nz + 1,)),
        dma((nz + 1,)),
        dma((ex_n,)),
        dma((ex_n,)),
        dma((2, far - 1, far)),
        dma((2, far - 1, far)),
        dma((2, far - 1)),
        dma((2, far - 1)),
        dma((nz - 1,)),
        dma((nz - 1,)),
        dma((ex_n,)),
        dma((ex_n,)),
    ]
    anywhere = pl.BlockSpec(memory_space=pl.ANY)
    local = pl.BlockSpec(memory_space=pltpu.VMEM)
    return pl.pallas_call(
        functools.partial(kernel, ny, nx, nz, groups, rank),
        out_shape=(
            jax.ShapeDtypeStruct((count, 256), BF16),
            jax.ShapeDtypeStruct((count, 256), F32),
        ),
        in_specs=[anywhere, anywhere, pl.BlockSpec(memory_space=pltpu.SMEM), anywhere, anywhere],
        out_specs=(local, local),
        scratch_shapes=scratch,
        compiler_params=pltpu.CompilerParams(
            collective_id=0, has_side_effects=True, vmem_limit_bytes=56 * 1024 * 1024
        ),
        cost_estimate=pl.CostEstimate(
            flops=4_000_000_000, bytes_accessed=13_000_000, transcendentals=0
        ),
    )(adapter_inputs, output_gradient, lengths, projection, validation)


def solution(mesh):
    ex_n, par_n = mesh.shape["ex"], mesh.shape["par"]
    nx = 1
    while nx * nx < ex_n:
        nx *= 2
    in_specs = (
        P("ex", None, None),
        P("ex", None, "par"),
        P("ex"),
        P(("par", "ex"), None),
        P("par", "ex"),
    )
    out_specs = (P("par", "ex"), P("par", "ex"))
    return jax.shard_map(
        functools.partial(shards, ex_n // nx, nx, par_n // 2),
        mesh=mesh,
        in_specs=in_specs,
        out_specs=out_specs,
        check_vma=False,
    )
```

time: 532 us -> 73.6 us (0.14)
  waiting for transfers between devices: 395 us -> 0 us
  blocking collectives: 100 us -> 0 us
  Pallas kernels: 0 us -> 67.6 us
  between operations: 15.6 us -> 0.64 us
  matrix products: 14.4 us -> 0 us
    reduce_scatter x2 -> x0, waiting for transfers between devices: 394 us -> none  [the longest x1 394 us: shards(): lax.psum_scatter(stacked, ('ex', 'par'), scatter_dimension=0, tiled=True)]
    psum x1 -> x0, blocking collectives: 79.1 us -> none  [shards(): feat_all, val_all = lax.psum((feat_vector, val_vector), ('ex', 'par'))]
    pallas_call x0 -> x1, Pallas kernels: none -> 67.6 us  [shards(): pl.pallas_call(functools.partial(kernel, ny, nx, nz, groups, rank), out_s...]
    all_to_all x1 -> x0, blocking collectives: 20.9 us -> none  [shards(): lax.all_to_all(blocks, 'ex', split_axis=1, concat_axis=0, tiled=True)]
    dot_general x3 -> x0, matrix products: 14.4 us -> none  [the longest x1 8.68 us: shards(): jnp.einsum('ek,kjc->jec', gathered, column_view, preferred_element_type=j...]
  transfers between devices with their start and end apart: 3 -> 0, of which waited for: 1 -> 0; matrix products, arithmetic and copies ran while one was open for 0% -> 0% of each run, Pallas kernels for 0% -> 0%
where the time goes in v1:
time: 73.6 us; the launch traced here: 73.4 us
  Pallas kernels  67.6 us (92%)
  local copies, waits for them, and re-layouts  5.13 us (7%)
    pallas_call x1, Pallas kernels, shards(): pl.pallas_call(functools.partial(kernel, ny, nx, nz, groups, rank), out_s...  67.6 us
    unnamed x3, local copies, waits for them, and re-layouts  5.13 us

profile of v1, /device:TPU:1, one launch (start us, length us, event | category | flops | bytes accessed | tf_op | source)
XLA Modules:
  0.0 73.4 jit_solution(5049948082187815634)
XLA Ops:
  0.6 2.5 %copy.7.ai_hbm = bf16[24,256,64]{2,1,0:T(8,128)(2,1)} copy(bf16[24,256,64]{1,2,0:T(8,128)(2,1)} %param.5) | data formatting | bytes 1572864 | tf_op args[0]
  3.1 67.6 %shard_map.68 = (bf16[24,256]{1,0:T(8,128)(2,1)}, f32[24,256]{1,0:T(8,128)}) custom-call(bf16[24,256,64]{2,1,0:T(8,128)(2,1)} %copy.7.ai_hbm, bf16[24,256,256]{2,1,0:T(8,128)(2,1)} %og_hbm.1, s32[24]{0:T(128)} %len_ref.1, bf16[1024,4096]{1,0:T(8,128)(2,1)} %proj_hbm.1, bf16[256,256]{1,0:T(8,128)(2,1)} %val_hbm.1), custom_call_target="tpu_custom_call" | custom-call | flops 4000000000 | bytes 13000000 | tf_op jit(solution)/shard_map/pallas_call | solution.py:483
  70.7 1.3 %copy.10 = bf16[24,256]{1,0:T(8,128)(2,1)} copy(bf16[24,256]{1,0:T(8,128)(2,1)} %get-tuple-element.4) | data formatting | bytes 24576
  72.0 1.3 %copy.11 = f32[24,256]{1,0:T(8,128)} copy(f32[24,256]{1,0:T(8,128)} %get-tuple-element.5) | data formatting | bytes 49152

commit v2 on v1

v2 whole, which is shorter than its diff:
```python
import functools

import jax
import jax.numpy as jnp
from jax import lax
from jax.experimental import pallas as pl
from jax.experimental.pallas import tpu as pltpu
from jax.sharding import PartitionSpec as P

MESH = pl.DeviceIdType.MESH
F32 = jnp.float32
BF16 = jnp.bfloat16


def kernel(
    ny, nx, nz, groups, rank,
    ai_hbm, og_hbm, len_ref, proj_hbm, val_hbm,
    feat_ref, score_ref,
    ai_v, og_v, proj_v, val_v, stage_v, send_a, recv_a, lhs, prod, recv_c,
    send_x, recv_x, keep_x, send_y, recv_y, keep_y, send_2, recv_2, keep_2,
    send_3, recv_3, val_sq, send_d, recv_d,
    ai_sem, og_sem, proj_sem, val_sem,
    as_sem, ar_sem, vs_sem, vr_sem, ws_sem, wr_sem, cs_sem, cr_sem,
    sx_sem, rx_sem, sy_sem, ry_sem, s2_sem, r2_sem, s3_sem, r3_sem, ds_sem, dr_sem,
):
    ex_n = ny * nx
    ex = lax.axis_index("ex")
    par = lax.axis_index("par")
    y, x = lax.div(ex, nx), lax.rem(ex, nx)
    z, core = lax.div(par, 2), lax.rem(par, 2)
    tokens = ai_v.shape[2]
    half_z = nz // 2

    def plane(oy, ox):
        return lax.rem(y + oy, ny) * nx + lax.rem(x + ox, nx)

    def depth(oz):
        return lax.rem(z + oz + nz, nz)

    def remote(src, dst, ssem, rsem, to_ex, to_par):
        return pltpu.make_async_remote_copy(
            src_ref=src, dst_ref=dst, send_sem=ssem, recv_sem=rsem,
            device_id=(to_ex, to_par), device_id_type=MESH,
        )

    for g in range(groups):
        rows = pl.ds(g * 8, 8)
        pltpu.make_async_copy(ai_hbm.at[rows], ai_v.at[rows], ai_sem.at[g]).start()
        pltpu.make_async_copy(og_hbm.at[rows], og_v.at[rows], og_sem.at[g]).start()
    val_copy = pltpu.make_async_copy(val_hbm, val_v.at[par], val_sem)
    val_copy.start()

    def proj_copy(s, q):
        return pltpu.make_async_copy(
            proj_hbm.at[pl.ds((q * 8 + s) * rank, rank)],
            proj_v.at[pl.ds(s * 2 * rank + q * rank, rank)],
            proj_sem.at[s, q],
        )

    for s in range(8):
        for q in range(2):
            proj_copy(s, q).start()

    barrier = pltpu.get_barrier_semaphore()

    def greet(to_ex, to_par):
        pl.semaphore_signal(barrier, inc=1, device_id=(to_ex, to_par), device_id_type=MESH)

    def greet_plane(o, _):
        greet(plane(lax.div(o, nx), lax.rem(o, nx)), par)
        return 0

    lax.fori_loop(1, ex_n, greet_plane, 0)

    def greet_depth(o, _):
        greet(ex, depth(o) * 2 + core)
        return 0

    lax.fori_loop(1, nz, greet_depth, 0)
    greet(ex, z * 2 + 1 - core)

    ring_plus, ring_minus = nz // 2, (nz - 1) // 2

    def val_hop(k, sign):
        slot = depth(-sign * (k - 1)) * 2 + core
        sem = k if sign > 0 else ring_plus + k
        return remote(
            val_v.at[slot], val_v.at[slot], vs_sem.at[sem], vr_sem.at[sem], ex, depth(sign) * 2 + core
        )

    def val_cross(k, sign):
        slot = depth(-sign * k) * 2 + core
        sem = k if sign > 0 else ring_plus + k
        return remote(
            val_v.at[slot], val_v.at[slot], ws_sem.at[sem], wr_sem.at[sem], ex, z * 2 + 1 - core
        )

    def val_point(k):
        if k == 0:
            val_copy.wait()
            val_cross(0, 1).start()
        else:
            if k <= ring_plus:
                val_hop(k, 1).wait_recv()
                val_cross(k, 1).start()
            if k <= ring_minus:
                val_hop(k, -1).wait_recv()
                val_cross(k, -1).start()
        if k + 1 <= ring_plus:
            val_hop(k + 1, 1).start()
        if k + 1 <= ring_minus:
            val_hop(k + 1, -1).start()

    lane = lax.broadcasted_iota(jnp.int32, (ex_n, 8, 128), 2)

    def a2a(g, o):
        to = plane(lax.div(o, nx), lax.rem(o, nx))
        return remote(
            send_a.at[g, to], recv_a.at[g, ex], as_sem.at[g, o], ar_sem.at[g, o], to, par
        )

    for g in range(groups):
        rows = pl.ds(g * 8, 8)
        pltpu.make_async_copy(ai_hbm.at[rows], ai_v.at[rows], ai_sem.at[g]).wait()
        pltpu.make_async_copy(og_hbm.at[rows], og_v.at[rows], og_sem.at[g]).wait()

        def gradient(e, _, g=g):
            m = g * 8 + e
            live = lax.broadcasted_iota(jnp.int32, (rank, tokens), 1) < len_ref[m]
            acts = jnp.where(live, ai_v[m].astype(F32), 0.0).astype(BF16)
            out = lax.dot_general(
                og_v[m], jnp.concatenate([acts, acts], axis=0),
                (((0,), (1,)), ((), ())), preferred_element_type=F32,
            )
            out = out.reshape(ex_n, 2, 8, 2 * rank)
            both = jnp.where(lane < rank, out[:, 0], out[:, 1])
            stage_v[pl.ds(pl.multiple_of(e * ex_n * 8, ex_n * 8), ex_n * 8), :] = both.reshape(
                ex_n * 8, 2 * rank
            )
            return 0

        lax.fori_loop(0, 8, gradient, 0)

        def pack(j, _, g=g):
            for q in range(4):
                low = stage_v[pl.ds(j * 8 + q, 8, stride=ex_n * 8), :]
                high = stage_v[pl.ds(j * 8 + q + 4, 8, stride=ex_n * 8), :]
                send_a[g, j, :, q * 128 : (q + 1) * 128] = jnp.concatenate(
                    [low, high], axis=0
                ).astype(BF16)
            return 0

        lax.fori_loop(0, ex_n, pack, 0)
        recv_a[g, ex] = send_a[g, ex]
        if g == 0:
            pl.semaphore_wait(barrier, ex_n - 1 + nz - 1 + 1)

        def send(o, _, g=g):
            a2a(g, o).start()
            return 0

        lax.fori_loop(1, ex_n, send, 0)
        if g == 0:
            val_point(0)

    def row_of(u):
        return lax.rem(lax.rem(u, ny) + 1, ny)

    def core_copy(u):
        return remote(
            prod.at[u, 1 - core], recv_c.at[u], cs_sem.at[u], cr_sem.at[u], ex, z * 2 + 1 - core
        )

    def first_x(g, dy, dx):
        return remote(
            send_x.at[g, dy, dx - 1], recv_x.at[g, dy, dx - 1],
            sx_sem.at[g, dy, dx - 1], rx_sem.at[g, dy, dx - 1], plane(0, dx), par,
        )

    def first_y(g, dy):
        return remote(
            send_y.at[g, dy - 1], recv_y.at[g, dy - 1],
            sy_sem.at[g, dy - 1], ry_sem.at[g, dy - 1], plane(dy, 0), par,
        )

    def pass_on(u):
        g, dy = lax.div(u, ny), row_of(u)
        core_copy(u).wait_recv()
        for dx in [*range(1, nx), 0]:
            xx = lax.rem(x + dx, nx)
            total = prod[u, core, xx, 0:half_z] + recv_c[u, xx, 0:half_z]
            if dx == 0:
                keep_x[g, dy] = total
            else:
                send_x[g, dy, dx - 1] = total.astype(BF16)
                first_x(g, dy, dx).start()

        @pl.when(dy == 0)
        def _():
            for xx in range(nx):
                keep_y[g, xx] = prod[u, core, xx, half_z:nz] + recv_c[u, xx, half_z:nz]

        @pl.when(dy != 0)
        def _():
            for xx in range(nx):
                send_y[g, dy - 1, xx] = (
                    prod[u, core, xx, half_z:nz] + recv_c[u, xx, half_z:nz]
                ).astype(BF16)
            first_y(g, dy).start()

    def chunk(u, _):
        g = lax.div(u, ny)
        yy = lax.rem(y + row_of(u), ny)
        left = lhs[pl.ds(pl.multiple_of(g * ex_n * 8, 16), ex_n * 8), :]
        for xx in range(nx):
            out = jnp.dot(
                left, proj_v[:, pl.ds(pl.multiple_of((yy * nx + xx) * 256, 256), 256)],
                preferred_element_type=F32,
            )
            for l in range(2):
                part = out[:, l * 128 : (l + 1) * 128].reshape(nz, 2, 8, 128)
                for c in range(2):
                    prod[u, c, xx, :, l * 8 : (l + 1) * 8, :] = part[:, c]
        core_copy(u).start()

        @pl.when(u > 0)
        def _():
            pass_on(u - 1)

        return 0

    def second(part, g, o):
        to = plane(o, 0) if part == 0 else plane(0, o)
        return remote(
            send_2.at[part, g, o - 1], recv_2.at[part, g, o - 1],
            s2_sem.at[part, g, o - 1], r2_sem.at[part, g, o - 1], to, par,
        )

    def pass_second(g):
        for dy in range(1, ny):
            first_y(g, dy).wait_recv()
        for o in [*range(1, nx), 0]:
            for dx in range(1, nx):
                first_x(g, o, dx).wait_recv()
            acc = keep_x[g, o]
            for dx in range(1, nx):
                acc += recv_x[g, o, dx - 1].astype(F32)
            if o == 0:
                keep_2[0:half_z, g] = acc
            else:
                send_2[0, g, o - 1] = acc.astype(BF16)
                second(0, g, o).start()
            xx = lax.rem(x + o, nx)
            acc = keep_y[g, xx]
            for dy in range(1, ny):
                acc += recv_y[g, dy - 1, xx].astype(F32)
            if o == 0:
                keep_2[half_z:nz, g] = acc
            else:
                send_2[1, g, o - 1] = acc.astype(BF16)
                second(1, g, o).start()

    def end_second(g):
        for part in range(2):
            own = slice(0, half_z) if part == 0 else slice(half_z, nz)
            acc = keep_2[own, g]
            for o in range(1, nx):
                second(part, g, o).wait_recv()
                acc += recv_2[part, g, o - 1].astype(F32)
            keep_2[own, g] = acc
            send_3[own, g] = acc.astype(BF16)

    ones = jnp.ones((16, 256), BF16)

    def val_norm(b, _):
        wide = val_v[b].astype(F32)
        sq = wide * wide
        high = sq.astype(BF16)
        low = (sq - high.astype(F32)).astype(BF16)
        dims = (((1,), (1,)), ((), ()))
        val_sq[b] = (
            lax.dot_general(ones, high, dims, preferred_element_type=F32)
            + lax.dot_general(ones, low, dims, preferred_element_type=F32)
        )[0:8]
        return 0

    for g in range(groups):
        def arrive(o, _, g=g):
            a2a(g, o).wait_recv()
            return 0

        lax.fori_loop(1, ex_n, arrive, 0)

        def gather(t, _, g=g):
            pair = recv_a[g, pl.ds(2 * t, 2)].astype(F32)
            place = pl.ds(pl.multiple_of(g * ex_n * 8 + t * 16, 16), 16)
            for h in range(2):
                lhs[place, h * 512 : (h + 1) * 512] = jnp.concatenate(
                    [pair[0, h * 8 : h * 8 + 8], pair[1, h * 8 : h * 8 + 8]], axis=0
                ).astype(BF16)
            return 0

        lax.fori_loop(0, ex_n // 2, gather, 0)
        if g == 0:
            for s in range(8):
                for q in range(2):
                    proj_copy(s, q).wait()
        if g + 1 <= ring_plus:
            val_point(g + 1)
        lax.fori_loop(g * ny, (g + 1) * ny, chunk, 0)
        if g >= 1:
            pass_second(g - 1)
    pass_on(groups * ny - 1)
    for k in range(groups + 1, ring_plus + 1):
        val_point(k)
    for k in range(ring_plus + 1):
        val_cross(k, 1).wait_recv()
        if 1 <= k <= ring_minus:
            val_cross(k, -1).wait_recv()
    lax.fori_loop(0, val_v.shape[0], val_norm, 0)
    pass_second(groups - 1)
    for g in range(groups):
        end_second(g)

    def third(o):
        return remote(
            send_3.at[depth(o)], recv_3.at[o - 1], s3_sem.at[o - 1], r3_sem.at[o - 1],
            ex, depth(o) * 2 + core,
        )

    def start_third(o, _):
        third(o).start()
        return 0

    lax.fori_loop(1, nz, start_third, 0)
    acc = keep_2[z]
    for o in range(1, nz):
        third(o).wait_recv()
        acc += recv_3[o - 1].astype(F32)
    rows = groups * 8
    wide = jnp.concatenate(
        [
            jnp.concatenate([acc[g, l * 8 : (l + 1) * 8] for g in range(groups)], axis=0)
            for l in range(2)
        ],
        axis=1,
    )
    features = wide.astype(BF16)
    feat_ref[...] = features

    rounded = features.astype(F32)
    column = jnp.sum(rounded * rounded, axis=1, keepdims=True)
    diagonal = lax.broadcasted_iota(jnp.int32, (rows, 256), 0) == lax.broadcasted_iota(
        jnp.int32, (rows, 256), 1
    )
    feat_row = jnp.sum(jnp.where(diagonal, column, 0.0), axis=0, keepdims=True)
    padded = jnp.concatenate([rounded, jnp.zeros((8, 256), F32)], axis=0).astype(BF16)
    sub = lax.broadcasted_iota(jnp.int32, (8, 256), 0)

    def split(row):
        first = row.astype(BF16).astype(F32)
        second_ = (row - first).astype(BF16).astype(F32)
        return first, second_, row - first - second_

    feat_rows = split(feat_row)

    def dots_copy(o):
        to = plane(lax.div(o, nx), lax.rem(o, nx))
        return remote(
            send_d.at[to], recv_d.at[o], ds_sem.at[o], dr_sem.at[o], to, par
        )

    def dots(o, _):
        b = plane(lax.div(o, nx), lax.rem(o, nx))
        part = lax.dot_general(
            padded, val_v[b], (((1,), (1,)), ((), ())), preferred_element_type=F32
        )
        extra = jnp.zeros((8, 256), F32)
        for k, row in enumerate((*split(val_sq[b]), *feat_rows)):
            extra = jnp.where(sub == k, row, extra)
        send_d[b] = jnp.concatenate([part[0:rows], extra], axis=0).astype(BF16)

        @pl.when(o != 0)
        def _():
            dots_copy(o).start()

        return 0

    lax.fori_loop(0, ex_n, dots, 0)

    def add_dots(o, total):
        dots_copy(o).wait_recv()
        return total + recv_d[o].astype(F32)

    total = lax.fori_loop(1, ex_n, add_dots, send_d[ex].astype(F32))
    val_row = total[rows : rows + 1] + total[rows + 1 : rows + 2] + total[rows + 2 : rows + 3]
    feat_row = total[rows + 3 : rows + 4] + total[rows + 4 : rows + 5] + total[rows + 5 : rows + 6]
    feat_sq = jnp.sum(jnp.where(diagonal, feat_row, 0.0), axis=1, keepdims=True)
    factor = float(256 * ex_n) ** 0.5
    score_ref[...] = (
        factor * total[0:rows] * lax.rsqrt(feat_sq + 1e-06) * lax.rsqrt(val_row + 1e-06)
    )

    def sent_plane(o, _):
        for g in range(groups):
            a2a(g, o).wait_send()
        dots_copy(o).wait_send()
        return 0

    lax.fori_loop(1, ex_n, sent_plane, 0)

    def sent_core(u, _):
        core_copy(u).wait_send()
        return 0

    lax.fori_loop(0, groups * ny, sent_core, 0)
    for k in range(ring_plus + 1):
        val_cross(k, 1).wait_send()
        if k >= 1:
            val_hop(k, 1).wait_send()
        if 1 <= k <= ring_minus:
            val_cross(k, -1).wait_send()
            val_hop(k, -1).wait_send()
    for g in range(groups):
        for dx in range(1, nx):
            for dy in range(ny):
                first_x(g, dy, dx).wait_send()
        for dy in range(1, ny):
            first_y(g, dy).wait_send()
        for o in range(1, nx):
            second(0, g, o).wait_send()
            second(1, g, o).wait_send()
    for o in range(1, nz):
        third(o).wait_send()


def shards(ny, nx, nz, adapter_inputs, output_gradient, lengths, projection, validation):
    adapter_inputs = jnp.swapaxes(adapter_inputs, 1, 2)
    count, rank, tokens = adapter_inputs.shape
    width = output_gradient.shape[2]
    ex_n, par_n = ny * nx, nz * 2
    groups = count // 8
    vm, dma = pltpu.VMEM, pltpu.SemaphoreType.DMA
    half_z = nz // 2
    x_block, y_block = (half_z, 16, 128), (nx, half_z, 16, 128)
    scratch = [
        vm((count, rank, tokens), BF16),
        vm((count, tokens, width), BF16),
        vm(projection.shape, BF16),
        vm((par_n, 256, 256), BF16),
        vm((8 * ex_n * 8, 128), F32),
        vm((groups, ex_n, 16, 512), BF16),
        vm((groups, ex_n, 16, 512), BF16),
        vm((groups * ex_n * 8, 1024), BF16),
        vm((groups * ny, 2, nx, nz, 16, 128), F32),
        vm((groups * ny, nx, nz, 16, 128), F32),
        vm((groups, ny, nx - 1, *x_block), BF16),
        vm((groups, ny, nx - 1, *x_block), BF16),
        vm((groups, ny, *x_block), F32),
        vm((groups, ny - 1, *y_block), BF16),
        vm((groups, ny - 1, *y_block), BF16),
        vm((groups, *y_block), F32),
        vm((2, groups, nx - 1, *x_block), BF16),
        vm((2, groups, nx - 1, *x_block), BF16),
        vm((nz, groups, 16, 128), F32),
        vm((nz, groups, 16, 128), BF16),
        vm((nz - 1, groups, 16, 128), BF16),
        vm((par_n, 8, 256), F32),
        vm((ex_n, 32, 256), BF16),
        vm((ex_n, 32, 256), BF16),
        dma((groups,)),
        dma((groups,)),
        dma((8, 2)),
        dma(()),
        dma((groups, ex_n)),
        dma((groups, ex_n)),
        dma((nz + 1,)),
        dma((nz + 1,)),
        dma((nz + 1,)),
        dma((nz + 1,)),
        dma((groups * ny,)),
        dma((groups * ny,)),
        dma((groups, ny, nx - 1)),
        dma((groups, ny, nx - 1)),
        dma((groups, ny - 1)),
        dma((groups, ny - 1)),
        dma((2, groups, nx - 1)),
        dma((2, groups, nx - 1)),
        dma((nz - 1,)),
        dma((nz - 1,)),
        dma((ex_n,)),
        dma((ex_n,)),
    ]
    anywhere = pl.BlockSpec(memory_space=pl.ANY)
    local = pl.BlockSpec(memory_space=pltpu.VMEM)
    return pl.pallas_call(
        functools.partial(kernel, ny, nx, nz, groups, rank),
        out_shape=(
            jax.ShapeDtypeStruct((count, 256), BF16),
            jax.ShapeDtypeStruct((count, 256), F32),
        ),
        in_specs=[anywhere, anywhere, pl.BlockSpec(memory_space=pltpu.SMEM), anywhere, anywhere],
        out_specs=(local, local),
        scratch_shapes=scratch,
        compiler_params=pltpu.CompilerParams(
            collective_id=0, has_side_effects=True, vmem_limit_bytes=56 * 1024 * 1024
        ),
        cost_estimate=pl.CostEstimate(
            flops=4_000_000_000, bytes_accessed=13_000_000, transcendentals=0
        ),
    )(adapter_inputs, output_gradient, lengths, projection, validation)


def solution(mesh):
    ex_n, par_n = mesh.shape["ex"], mesh.shape["par"]
    nx = 1
    while nx * nx < ex_n:
        nx *= 2
    in_specs = (
        P("ex", None, None),
        P("ex", None, "par"),
        P("ex"),
        P(("par", "ex"), None),
        P("par", "ex"),
    )
    out_specs = (P("par", "ex"), P("par", "ex"))
    return jax.shard_map(
        functools.partial(shards, ex_n // nx, nx, par_n // 2),
        mesh=mesh,
        in_specs=in_specs,
        out_specs=out_specs,
        check_vma=False,
    )
```

time: 73.6 us -> 59.8 us (0.81)
  Pallas kernels: 67.6 us -> 56 us
  local copies, waits for them, and re-layouts: 5.13 us -> 2.65 us
    pallas_call x1, Pallas kernels: 67.6 us -> 56 us  [shards(): pl.pallas_call(functools.partial(kernel, ny, nx, nz, groups, rank), out_s...]
    unnamed x3 -> x2, local copies, waits for them, and re-layouts: 5.13 us -> 2.65 us
where the time goes in v2:
time: 59.8 us; the launch traced here: 59.3 us
  Pallas kernels  56 us (94%)
  local copies, waits for them, and re-layouts  2.65 us (4%)
  between operations  0.64 us (1%)
    pallas_call x1, Pallas kernels, shards(): pl.pallas_call(functools.partial(kernel, ny, nx, nz, groups, rank), out_s...  56 us
    unnamed x2, local copies, waits for them, and re-layouts  2.65 us

profile of v2, /device:TPU:1, one launch (start us, length us, event | category | flops | bytes accessed | tf_op | source)
XLA Modules:
  0.0 59.3 jit_solution(10821627943319897409)
XLA Ops:
  0.6 56.0 %shard_map.68 = (bf16[24,256]{1,0:T(8,128)(2,1)}, f32[24,256]{1,0:T(8,128)}) custom-call(bf16[24,64,256]{2,1,0:T(8,128)(2,1)} %bitcast.1, bf16[24,256,256]{2,1,0:T(8,128)(2,1)} %og_hbm.1, s32[24]{0:T(128)} %len_ref.1, bf16[1024,4096]{1,0:T(8,128)(2,1)} %proj_hbm.1, bf16[256,256]{1,0:T(8,128)(2,1)} %val_hbm.1), custom_call_target="tpu_custom_call" | custom-call | flops 4000000000 | bytes 13000000 | tf_op jit(solution)/shard_map/pallas_call | solution.py:496
  56.7 1.3 %copy.9 = bf16[24,256]{1,0:T(8,128)(2,1)} copy(bf16[24,256]{1,0:T(8,128)(2,1)} %get-tuple-element.4) | data formatting | bytes 24576
  58.0 1.3 %copy.10 = f32[24,256]{1,0:T(8,128)} copy(f32[24,256]{1,0:T(8,128)} %get-tuple-element.5) | data formatting | bytes 49152

commit v3 on v2

--- a/solution.py
+++ b/solution.py
@@ -14,12 +14,12 @@
 
 def kernel(
     ny, nx, nz, groups, rank,
-    ai_hbm, og_hbm, len_ref, proj_hbm, val_hbm,
-    feat_ref, score_ref,
-    ai_v, og_v, proj_v, val_v, stage_v, send_a, recv_a, lhs, prod, recv_c,
+    ai_hbm, og_hbm, len_hbm, proj_hbm, val_hbm,
+    out_ref,
+    len_ref, ai_v, og_v, proj_v, val_v, stage_v, send_a, recv_a, lhs, prod, recv_c,
     send_x, recv_x, keep_x, send_y, recv_y, keep_y, send_2, recv_2, keep_2,
     send_3, recv_3, val_sq, send_d, recv_d,
-    ai_sem, og_sem, proj_sem, val_sem,
+    len_sem, ai_sem, og_sem, proj_sem, val_sem,
     as_sem, ar_sem, vs_sem, vr_sem, ws_sem, wr_sem, cs_sem, cr_sem,
     sx_sem, rx_sem, sy_sem, ry_sem, s2_sem, r2_sem, s3_sem, r3_sem, ds_sem, dr_sem,
 ):
@@ -43,10 +43,38 @@
             device_id=(to_ex, to_par), device_id_type=MESH,
         )
 
-    for g in range(groups):
+    def load(g):
         rows = pl.ds(g * 8, 8)
+        pltpu.make_async_copy(og_hbm.at[rows], og_v.at[rows], og_sem.at[g]).start()
         pltpu.make_async_copy(ai_hbm.at[rows], ai_v.at[rows], ai_sem.at[g]).start()
-        pltpu.make_async_copy(og_hbm.at[rows], og_v.at[rows], og_sem.at[g]).start()
+
+    load(0)
+    len_copy = pltpu.make_async_copy(len_hbm, len_ref, len_sem)
+    len_copy.start()
+
+    barrier = pltpu.get_barrier_semaphore()
+
+    def greet(to_ex, to_par):
+        pl.semaphore_signal(barrier, inc=1, device_id=(to_ex, to_par), device_id_type=MESH)
+
+    def greet_plane(o, _):
+        greet(plane(lax.div(o, nx), lax.rem(o, nx)), par)
+        return 0
+
+    lax.fori_loop(1, ex_n, greet_plane, 0)
+
+    def greet_depth(o, _):
+        greet(ex, depth(o) * 2 + core)
+        return 0
+
+    lax.fori_loop(1, nz, greet_depth, 0)
+    greet(ex, z * 2 + 1 - core)
+
+    def whole(src, dst, ssem, rsem):
+        return remote(src, dst, ssem, rsem, ex, z * 2 + 1 - core)
+
+    for g in range(1, groups):
+        load(g)
     val_copy = pltpu.make_async_copy(val_hbm, val_v.at[par], val_sem)
     val_copy.start()
 
@@ -54,30 +82,8 @@
         return pltpu.make_async_copy(
             proj_hbm.at[pl.ds((q * 8 + s) * rank, rank)],
             proj_v.at[pl.ds(s * 2 * rank + q * rank, rank)],
-            proj_sem.at[s, q],
-        )
-
-    for s in range(8):
-        for q in range(2):
-            proj_copy(s, q).start()
-
-    barrier = pltpu.get_barrier_semaphore()
-
-    def greet(to_ex, to_par):
-        pl.semaphore_signal(barrier, inc=1, device_id=(to_ex, to_par), device_id_type=MESH)
-
-    def greet_plane(o, _):
-        greet(plane(lax.div(o, nx), lax.rem(o, nx)), par)
-        return 0
-
-    lax.fori_loop(1, ex_n, greet_plane, 0)
-
-    def greet_depth(o, _):
-        greet(ex, depth(o) * 2 + core)
-        return 0
-
-    lax.fori_loop(1, nz, greet_depth, 0)
-    greet(ex, z * 2 + 1 - core)
+            proj_sem,
+        )
 
     ring_plus, ring_minus = nz // 2, (nz - 1) // 2
 
@@ -85,14 +91,14 @@
         slot = depth(-sign * (k - 1)) * 2 + core
         sem = k if sign > 0 else ring_plus + k
         return remote(
-            val_v.at[slot], val_v.at[slot], vs_sem.at[sem], vr_sem.at[sem], ex, depth(sign) * 2 + core
+            val_v.at[slot], val_v.at[slot], vs_sem, vr_sem.at[sem], ex, depth(sign) * 2 + core
         )
 
     def val_cross(k, sign):
         slot = depth(-sign * k) * 2 + core
         sem = k if sign > 0 else ring_plus + k
         return remote(
-            val_v.at[slot], val_v.at[slot], ws_sem.at[sem], wr_sem.at[sem], ex, z * 2 + 1 - core
+            val_v.at[slot], val_v.at[slot], ws_sem, wr_sem.at[sem], ex, z * 2 + 1 - core
         )
 
     def val_point(k):
@@ -116,7 +122,7 @@
     def a2a(g, o):
         to = plane(lax.div(o, nx), lax.rem(o, nx))
         return remote(
-            send_a.at[g, to], recv_a.at[g, ex], as_sem.at[g, o], ar_sem.at[g, o], to, par
+            send_a.at[g, to], recv_a.at[g, ex], as_sem.at[g], ar_sem.at[g], to, par
         )
 
     for g in range(groups):
@@ -139,7 +145,9 @@
             )
             return 0
 
-        lax.fori_loop(0, 8, gradient, 0)
+        if g == 0:
+            len_copy.wait()
+        lax.fori_loop(0, 8, gradient, 0, unroll=4)
 
         def pack(j, _, g=g):
             for q in range(4):
@@ -150,7 +158,7 @@
                 ).astype(BF16)
             return 0
 
-        lax.fori_loop(0, ex_n, pack, 0)
+        lax.fori_loop(0, ex_n, pack, 0, unroll=4)
         recv_a[g, ex] = send_a[g, ex]
         if g == 0:
             pl.semaphore_wait(barrier, ex_n - 1 + nz - 1 + 1)
@@ -161,26 +169,31 @@
 
         lax.fori_loop(1, ex_n, send, 0)
         if g == 0:
+            for s in range(8):
+                for q in range(2):
+                    proj_copy(s, q).start()
             val_point(0)
+        if g == groups - 1:
+            val_point(1)
 
     def row_of(u):
         return lax.rem(lax.rem(u, ny) + 1, ny)
 
     def core_copy(u):
         return remote(
-            prod.at[u, 1 - core], recv_c.at[u], cs_sem.at[u], cr_sem.at[u], ex, z * 2 + 1 - core
+            prod.at[u, 1 - core], recv_c.at[u], cs_sem, cr_sem.at[u], ex, z * 2 + 1 - core
         )
 
     def first_x(g, dy, dx):
         return remote(
             send_x.at[g, dy, dx - 1], recv_x.at[g, dy, dx - 1],
-            sx_sem.at[g, dy, dx - 1], rx_sem.at[g, dy, dx - 1], plane(0, dx), par,
+            sx_sem, rx_sem.at[g, dy], plane(0, dx), par,
         )
 
     def first_y(g, dy):
         return remote(
             send_y.at[g, dy - 1], recv_y.at[g, dy - 1],
-            sy_sem.at[g, dy - 1], ry_sem.at[g, dy - 1], plane(dy, 0), par,
+            sy_sem, ry_sem.at[g], plane(dy, 0), par,
         )
 
     def pass_on(u):
@@ -222,26 +235,23 @@
                 for c in range(2):
                     prod[u, c, xx, :, l * 8 : (l + 1) * 8, :] = part[:, c]
         core_copy(u).start()
-
-        @pl.when(u > 0)
-        def _():
-            pass_on(u - 1)
-
+        return 0
+
+    def pass_group(u, _):
+        pass_on(u)
         return 0
 
     def second(part, g, o):
         to = plane(o, 0) if part == 0 else plane(0, o)
         return remote(
             send_2.at[part, g, o - 1], recv_2.at[part, g, o - 1],
-            s2_sem.at[part, g, o - 1], r2_sem.at[part, g, o - 1], to, par,
+            s2_sem, r2_sem.at[part, g], to, par,
         )
 
     def pass_second(g):
-        for dy in range(1, ny):
-            first_y(g, dy).wait_recv()
+        whole(send_y.at[g], recv_y.at[g], sy_sem, ry_sem.at[g]).wait_recv()
         for o in [*range(1, nx), 0]:
-            for dx in range(1, nx):
-                first_x(g, o, dx).wait_recv()
+            whole(send_x.at[g, o], recv_x.at[g, o], sx_sem, rx_sem.at[g, o]).wait_recv()
             acc = keep_x[g, o]
             for dx in range(1, nx):
                 acc += recv_x[g, o, dx - 1].astype(F32)
@@ -264,15 +274,17 @@
         for part in range(2):
             own = slice(0, half_z) if part == 0 else slice(half_z, nz)
             acc = keep_2[own, g]
+            whole(
+                send_2.at[part, g], recv_2.at[part, g], s2_sem, r2_sem.at[part, g]
+            ).wait_recv()
             for o in range(1, nx):
-                second(part, g, o).wait_recv()
                 acc += recv_2[part, g, o - 1].astype(F32)
             keep_2[own, g] = acc
             send_3[own, g] = acc.astype(BF16)
 
     ones = jnp.ones((16, 256), BF16)
 
-    def val_norm(b, _):
+    def val_norm(b):
         wide = val_v[b].astype(F32)
         sq = wide * wide
         high = sq.astype(BF16)
@@ -282,14 +294,19 @@
             lax.dot_general(ones, high, dims, preferred_element_type=F32)
             + lax.dot_general(ones, low, dims, preferred_element_type=F32)
         )[0:8]
-        return 0
+
+    def norms(k):
+        val_cross(k, 1).wait_recv()
+        if 1 <= k <= ring_minus:
+            val_cross(k, -1).wait_recv()
+        for c in range(2):
+            val_norm(depth(-k) * 2 + c)
+            if 1 <= k <= ring_minus:
+                val_norm(depth(k) * 2 + c)
 
     for g in range(groups):
-        def arrive(o, _, g=g):
-            a2a(g, o).wait_recv()
-            return 0
-
-        lax.fori_loop(1, ex_n, arrive, 0)
+        blocks = pl.ds(0, ex_n - 1)
+        whole(send_a.at[g, blocks], recv_a.at[g, blocks], as_sem.at[g], ar_sem.at[g]).wait_recv()
 
         def gather(t, _, g=g):
             pair = recv_a[g, pl.ds(2 * t, 2)].astype(F32)
@@ -302,29 +319,36 @@
 
         lax.fori_loop(0, ex_n // 2, gather, 0)
         if g == 0:
-            for s in range(8):
-                for q in range(2):
-                    proj_copy(s, q).wait()
-        if g + 1 <= ring_plus:
-            val_point(g + 1)
-        lax.fori_loop(g * ny, (g + 1) * ny, chunk, 0)
+            pltpu.make_async_copy(proj_hbm, proj_v, proj_sem).wait()
+        first = g * ny
+        ahead = min(2, ny)
+        lax.fori_loop(first, first + ahead, chunk, 0)
+
+        def both(u, _, ahead=ahead):
+            chunk(u, 0)
+            pass_on(u - ahead)
+            return 0
+
+        lax.fori_loop(first + ahead, first + ny, both, 0)
         if g >= 1:
             pass_second(g - 1)
-    pass_on(groups * ny - 1)
-    for k in range(groups + 1, ring_plus + 1):
+        lax.fori_loop(first + ny - ahead, first + ny, pass_group, 0)
+        if 2 <= g + 2 <= ring_plus:
+            val_point(g + 2)
+            norms(g)
+    done = min(groups, max(ring_plus - 1, 0))
+    pass_second(groups - 1)
+    for g in range(groups - 1):
+        end_second(g)
+    for k in range(max(groups + 2, 2), ring_plus + 1):
         val_point(k)
-    for k in range(ring_plus + 1):
-        val_cross(k, 1).wait_recv()
-        if 1 <= k <= ring_minus:
-            val_cross(k, -1).wait_recv()
-    lax.fori_loop(0, val_v.shape[0], val_norm, 0)
-    pass_second(groups - 1)
-    for g in range(groups):
-        end_second(g)
+    for k in range(done, ring_plus + 1):
+        norms(k)
+    end_second(groups - 1)
 
     def third(o):
         return remote(
-            send_3.at[depth(o)], recv_3.at[o - 1], s3_sem.at[o - 1], r3_sem.at[o - 1],
+            send_3.at[depth(o)], recv_3.at[o - 1], s3_sem, r3_sem,
             ex, depth(o) * 2 + core,
         )
 
@@ -333,9 +357,21 @@
         return 0
 
     lax.fori_loop(1, nz, start_third, 0)
+
+    for g in range(groups):
+        whole(send_a.at[g, blocks], recv_a.at[g, blocks], as_sem.at[g], ar_sem.at[g]).wait_send()
+    whole(prod.at[:, 0], recv_c, cs_sem, cr_sem.at[0]).wait_send()
+    hops, crosses = val_v.at[pl.ds(0, nz - 1)], val_v.at[pl.ds(0, nz)]
+    whole(hops, hops, vs_sem, vr_sem.at[0]).wait_send()
+    whole(crosses, crosses, ws_sem, wr_sem.at[0]).wait_send()
+    whole(send_x, recv_x, sx_sem, rx_sem.at[0, 0]).wait_send()
+    whole(send_y, recv_y, sy_sem, ry_sem.at[0]).wait_send()
+    whole(send_2, recv_2, s2_sem, r2_sem.at[0, 0]).wait_send()
+
+    last = whole(send_3.at[pl.ds(0, nz - 1)], recv_3, s3_sem, r3_sem)
+    last.wait_recv()
     acc = keep_2[z]
     for o in range(1, nz):
-        third(o).wait_recv()
         acc += recv_3[o - 1].astype(F32)
     rows = groups * 8
     wide = jnp.concatenate(
@@ -346,7 +382,7 @@
         axis=1,
     )
     features = wide.astype(BF16)
-    feat_ref[...] = features
+    out_ref[0] = features.astype(F32)
 
     rounded = features.astype(F32)
     column = jnp.sum(rounded * rounded, axis=1, keepdims=True)
@@ -367,11 +403,11 @@
     def dots_copy(o):
         to = plane(lax.div(o, nx), lax.rem(o, nx))
         return remote(
-            send_d.at[to], recv_d.at[o], ds_sem.at[o], dr_sem.at[o], to, par
-        )
-
-    def dots(o, _):
-        b = plane(lax.div(o, nx), lax.rem(o, nx))
+            send_d.at[to], recv_d.at[o], ds_sem, dr_sem, to, par
+        )
+
+    for o in [*range(ex_n - 1, 0, -1), 0]:
+        b = plane(o // nx, o % nx)
         part = lax.dot_general(
             padded, val_v[b], (((1,), (1,)), ((), ())), preferred_element_type=F32
         )
@@ -379,60 +415,26 @@
         for k, row in enumerate((*split(val_sq[b]), *feat_rows)):
             extra = jnp.where(sub == k, row, extra)
         send_d[b] = jnp.concatenate([part[0:rows], extra], axis=0).astype(BF16)
-
-        @pl.when(o != 0)
-        def _():
+        if o != 0:
             dots_copy(o).start()
 
-        return 0
-
-    lax.fori_loop(0, ex_n, dots, 0)
-
-    def add_dots(o, total):
-        dots_copy(o).wait_recv()
-        return total + recv_d[o].astype(F32)
-
-    total = lax.fori_loop(1, ex_n, add_dots, send_d[ex].astype(F32))
+    total = send_d[ex].astype(F32)
+    every = whole(
+        send_d.at[pl.ds(0, ex_n - 1)], recv_d.at[pl.ds(1, ex_n - 1)], ds_sem, dr_sem
+    )
+    every.wait_recv()
+    for o in range(1, ex_n):
+        total = total + recv_d[o].astype(F32)
     val_row = total[rows : rows + 1] + total[rows + 1 : rows + 2] + total[rows + 2 : rows + 3]
     feat_row = total[rows + 3 : rows + 4] + total[rows + 4 : rows + 5] + total[rows + 5 : rows + 6]
     feat_sq = jnp.sum(jnp.where(diagonal, feat_row, 0.0), axis=1, keepdims=True)
     factor = float(256 * ex_n) ** 0.5
-    score_ref[...] = (
+    out_ref[1] = (
         factor * total[0:rows] * lax.rsqrt(feat_sq + 1e-06) * lax.rsqrt(val_row + 1e-06)
     )
 
-    def sent_plane(o, _):
-        for g in range(groups):
-            a2a(g, o).wait_send()
-        dots_copy(o).wait_send()
-        return 0
-
-    lax.fori_loop(1, ex_n, sent_plane, 0)
-
-    def sent_core(u, _):
-        core_copy(u).wait_send()
-        return 0
-
-    lax.fori_loop(0, groups * ny, sent_core, 0)
-    for k in range(ring_plus + 1):
-        val_cross(k, 1).wait_send()
-        if k >= 1:
-            val_hop(k, 1).wait_send()
-        if 1 <= k <= ring_minus:
-            val_cross(k, -1).wait_send()
-            val_hop(k, -1).wait_send()
-    for g in range(groups):
-        for dx in range(1, nx):
-            for dy in range(ny):
-                first_x(g, dy, dx).wait_send()
-        for dy in range(1, ny):
-            first_y(g, dy).wait_send()
-        for o in range(1, nx):
-            second(0, g, o).wait_send()
-            second(1, g, o).wait_send()
-    for o in range(1, nz):
-        third(o).wait_send()
-
+    every.wait_send()
+    last.wait_send()
 
 def shards(ny, nx, nz, adapter_inputs, output_gradient, lengths, projection, validation):
     adapter_inputs = jnp.swapaxes(adapter_inputs, 1, 2)
@@ -444,6 +446,7 @@
     half_z = nz // 2
     x_block, y_block = (half_z, 16, 128), (nx, half_z, 16, 128)
     scratch = [
+        pltpu.SMEM(lengths.shape, jnp.int32),
         vm((count, rank, tokens), BF16),
         vm((count, tokens, width), BF16),
         vm(projection.shape, BF16),
@@ -468,39 +471,37 @@
         vm((par_n, 8, 256), F32),
         vm((ex_n, 32, 256), BF16),
         vm((ex_n, 32, 256), BF16),
+        dma(()),
         dma((groups,)),
         dma((groups,)),
-        dma((8, 2)),
-        dma(()),
-        dma((groups, ex_n)),
-        dma((groups, ex_n)),
-        dma((nz + 1,)),
-        dma((nz + 1,)),
-        dma((nz + 1,)),
-        dma((nz + 1,)),
+        dma(()),
+        dma(()),
+        dma((groups,)),
+        dma((groups,)),
+        dma(()),
+        dma((nz,)),
+        dma(()),
+        dma((nz,)),
+        dma(()),
         dma((groups * ny,)),
-        dma((groups * ny,)),
-        dma((groups, ny, nx - 1)),
-        dma((groups, ny, nx - 1)),
-        dma((groups, ny - 1)),
-        dma((groups, ny - 1)),
-        dma((2, groups, nx - 1)),
-        dma((2, groups, nx - 1)),
-        dma((nz - 1,)),
-        dma((nz - 1,)),
-        dma((ex_n,)),
-        dma((ex_n,)),
+        dma(()),
+        dma((groups, ny)),
+        dma(()),
+        dma((groups,)),
+        dma(()),
+        dma((2, groups)),
+        dma(()),
+        dma(()),
+        dma(()),
+        dma(()),
     ]
     anywhere = pl.BlockSpec(memory_space=pl.ANY)
     local = pl.BlockSpec(memory_space=pltpu.VMEM)
-    return pl.pallas_call(
+    out = pl.pallas_call(
         functools.partial(kernel, ny, nx, nz, groups, rank),
-        out_shape=(
-            jax.ShapeDtypeStruct((count, 256), BF16),
-            jax.ShapeDtypeStruct((count, 256), F32),
-        ),
-        in_specs=[anywhere, anywhere, pl.BlockSpec(memory_space=pltpu.SMEM), anywhere, anywhere],
-        out_specs=(local, local),
+        out_shape=jax.ShapeDtypeStruct((2, count, 256), F32),
+        in_specs=[anywhere, anywhere, anywhere, anywhere, anywhere],
+        out_specs=local,
         scratch_shapes=scratch,
         compiler_params=pltpu.CompilerParams(
             collective_id=0, has_side_effects=True, vmem_limit_bytes=56 * 1024 * 1024
@@ -509,6 +510,7 @@
             flops=4_000_000_000, bytes_accessed=13_000_000, transcendentals=0
         ),
     )(adapter_inputs, output_gradient, lengths, projection, validation)
+    return out[0].astype(BF16), out[1]
 
 
 def solution(mesh):

time: 59.8 us -> 54.4 us (0.910)
  Pallas kernels: 56 us -> 50.4 us
    pallas_call x1, Pallas kernels: 56 us -> 50.4 us  [shards(): pl.pallas_call(functools.partial(kernel, ny, nx, nz, groups, rank), out_s...]
    unnamed x2 -> x0, local copies, waits for them, and re-layouts: 2.65 us -> none
    squeeze x0 -> x1, local copies, waits for them, and re-layouts: none -> 1.35 us  [shards(): return (out[0].astype(BF16), out[1])]
    convert_element_type x0 -> x1, local copies, waits for them, and re-layouts: none -> 1.34 us  [shards(): return (out[0].astype(BF16), out[1])]
where the time goes in v3:
time: 54.4 us; the launch traced here: 53.7 us
  Pallas kernels  50.4 us (93%)
  local copies, waits for them, and re-layouts  2.69 us (5%)
  between operations  0.64 us (1%)
    pallas_call x1, Pallas kernels, shards(): pl.pallas_call(functools.partial(kernel, ny, nx, nz, groups, rank), out_s...  50.4 us
    squeeze x1, local copies, waits for them, and re-layouts, shards(): return (out[0].astype(BF16), out[1])  1.35 us
    convert_element_type x1, local copies, waits for them, and re-layouts, shards(): return (out[0].astype(BF16), out[1])  1.34 us

profile of v3, /device:TPU:1, one launch (start us, length us, event | category | flops | bytes accessed | tf_op | source)
XLA Modules:
  0.0 53.7 jit_solution(8885701828642363542)
XLA Ops:
  0.6 50.4 %shard_map.68 = f32[2,24,256]{2,1,0:T(8,128)} custom-call(bf16[24,64,256]{2,1,0:T(8,128)(2,1)} %bitcast.5, bf16[24,256,256]{2,1,0:T(8,128)(2,1)} %og_hbm.1, s32[24]{0:T(128)} %len_hbm.1, bf16[1024,4096]{1,0:T(8,128)(2,1)} %proj_hbm.1, bf16[256,256]{1,0:T(8,128)(2,1)} %val_hbm.1), custom_call_target="tpu_custom_call" | custom-call | flops 4000000000 | bytes 13000000 | tf_op jit(solution)/shard_map/pallas_call | solution.py:500
  51.0 1.3 %fusion = bf16[24,256]{1,0:T(8,128)(2,1)} fusion(f32[2,24,256]{2,1,0:T(8,128)} %shard_map.68), kind=kLoop, calls=%fused_computation.2 | loop fusion | bytes 24576 | tf_op jit(solution)/shard_map/convert_element_type | solution.py:513
  52.3 1.3 %slice_bitcast_fusion = f32[24,256]{1,0:T(8,128)} fusion(f32[2,24,256]{2,1,0:T(8,128)} %shard_map.68), kind=kLoop, calls=%fused_computation.1 | loop fusion | bytes 49152 | tf_op jit(solution)/shard_map/squeeze | solution.py:513

commit v4 on v3

--- a/solution.py
+++ b/solution.py
@@ -57,17 +57,11 @@
     def greet(to_ex, to_par):
         pl.semaphore_signal(barrier, inc=1, device_id=(to_ex, to_par), device_id_type=MESH)
 
-    def greet_plane(o, _):
-        greet(plane(lax.div(o, nx), lax.rem(o, nx)), par)
-        return 0
-
-    lax.fori_loop(1, ex_n, greet_plane, 0)
-
-    def greet_depth(o, _):
+    for o in range(1, ex_n):
+        greet(plane(o // nx, o % nx), par)
+
+    for o in range(1, nz):
         greet(ex, depth(o) * 2 + core)
-        return 0
-
-    lax.fori_loop(1, nz, greet_depth, 0)
     greet(ex, z * 2 + 1 - core)
 
     def whole(src, dst, ssem, rsem):
@@ -120,7 +114,7 @@
     lane = lax.broadcasted_iota(jnp.int32, (ex_n, 8, 128), 2)
 
     def a2a(g, o):
-        to = plane(lax.div(o, nx), lax.rem(o, nx))
+        to = plane(o // nx, o % nx)
         return remote(
             send_a.at[g, to], recv_a.at[g, ex], as_sem.at[g], ar_sem.at[g], to, par
         )
@@ -163,11 +157,8 @@
         if g == 0:
             pl.semaphore_wait(barrier, ex_n - 1 + nz - 1 + 1)
 
-        def send(o, _, g=g):
+        for o in range(1, ex_n):
             a2a(g, o).start()
-            return 0
-
-        lax.fori_loop(1, ex_n, send, 0)
         if g == 0:
             for s in range(8):
                 for q in range(2):
@@ -321,7 +312,7 @@
         if g == 0:
             pltpu.make_async_copy(proj_hbm, proj_v, proj_sem).wait()
         first = g * ny
-        ahead = min(2, ny)
+        ahead = min(3, ny)
         lax.fori_loop(first, first + ahead, chunk, 0)
 
         def both(u, _, ahead=ahead):
@@ -330,9 +321,9 @@
             return 0
 
         lax.fori_loop(first + ahead, first + ny, both, 0)
+        lax.fori_loop(first + ny - ahead, first + ny, pass_group, 0)
         if g >= 1:
             pass_second(g - 1)
-        lax.fori_loop(first + ny - ahead, first + ny, pass_group, 0)
         if 2 <= g + 2 <= ring_plus:
             val_point(g + 2)
             norms(g)
@@ -352,11 +343,8 @@
             ex, depth(o) * 2 + core,
         )
 
-    def start_third(o, _):
+    for o in range(1, nz):
         third(o).start()
-        return 0
-
-    lax.fori_loop(1, nz, start_third, 0)
 
     for g in range(groups):
         whole(send_a.at[g, blocks], recv_a.at[g, blocks], as_sem.at[g], ar_sem.at[g]).wait_send()
@@ -401,7 +389,7 @@
     feat_rows = split(feat_row)
 
     def dots_copy(o):
-        to = plane(lax.div(o, nx), lax.rem(o, nx))
+        to = plane(o // nx, o % nx)
         return remote(
             send_d.at[to], recv_d.at[o], ds_sem, dr_sem, to, par
         )
@@ -504,7 +492,7 @@
         out_specs=local,
         scratch_shapes=scratch,
         compiler_params=pltpu.CompilerParams(
-            collective_id=0, has_side_effects=True, vmem_limit_bytes=56 * 1024 * 1024
+            collective_id=0, has_side_effects=True, vmem_limit_bytes=55091 * 1024
         ),
         cost_estimate=pl.CostEstimate(
             flops=4_000_000_000, bytes_accessed=13_000_000, transcendentals=0

time: 54.4 us -> 51.4 us (0.945)
  Pallas kernels: 50.4 us -> 48 us
  local copies, waits for them, and re-layouts: 2.69 us -> 1.86 us
    pallas_call x1, Pallas kernels: 50.4 us -> 48 us  [shards(): pl.pallas_call(functools.partial(kernel, ny, nx, nz, groups, rank), out_s...]
    convert_element_type x1, local copies, waits for them, and re-layouts: 1.34 us -> 0.6 us  [shards(): return (out[0].astype(BF16), out[1])]
    squeeze x1, local copies, waits for them, and re-layouts: 1.35 us -> 0.61 us  [shards(): return (out[0].astype(BF16), out[1])]
    unnamed x0 -> x2, local copies, waits for them, and re-layouts: none -> 0.65 us
where the time goes in v4:
time: 51.4 us; the launch traced here: 50.5 us
  Pallas kernels  48 us (93%)
  local copies, waits for them, and re-layouts  1.86 us (4%)
  between operations  0.65 us (1%)
    pallas_call x1, Pallas kernels, shards(): pl.pallas_call(functools.partial(kernel, ny, nx, nz, groups, rank), out_s...  48 us

profile of v4, /device:TPU:1, one launch (start us, length us, event | category | flops | bytes accessed | tf_op | source)
XLA Modules:
  0.0 50.5 jit_solution(11757032674494647850)
XLA Ops:
  0.6 0.0 copy-start
  0.6 0.6 %copy-done = s32[24]{0:T(128)S(1)} copy-done((s32[24]{0:T(128)S(1)}, s32[24]{0:T(128)}, u32[]{:S(2)}) %copy-start) | copy-done | bytes 120
  1.3 48.0 %shard_map.68 = f32[2,24,256]{2,1,0:T(8,128)S(1)} custom-call(bf16[24,64,256]{2,1,0:T(8,128)(2,1)} %bitcast.5, bf16[24,256,256]{2,1,0:T(8,128)(2,1)} %og_hbm.1, s32[24]{0:T(128)S(1)} %copy-done, bf16[1024,4096]{1,0:T(8,128)(2,1)} %proj_hbm.1, bf16[256,256]{1,0:T(8,128)(2,1)} %val_hbm.1), custom_call_target="tpu_custom_call" | custom-call | flops 4000000000 | bytes 13000000 | tf_op jit(solution)/shard_map/pallas_call | solution.py:488
  49.3 0.6 %fusion = bf16[24,256]{1,0:T(8,128)(2,1)} fusion(f32[2,24,256]{2,1,0:T(8,128)S(1)} %shard_map.68), kind=kLoop, calls=%fused_computation.2 | loop fusion | bytes 24576 | tf_op jit(solution)/shard_map/convert_element_type | solution.py:501
  49.9 0.6 %slice_bitcast_fusion = f32[24,256]{1,0:T(8,128)} fusion(f32[2,24,256]{2,1,0:T(8,128)S(1)} %shard_map.68), kind=kLoop, calls=%fused_computation.1 | loop fusion | bytes 49152 | tf_op jit(solution)/shard_map/squeeze | solution.py:501
Async XLA Ops:
  0.6 0.7 %copy-start = (s32[24]{0:T(128)S(1)}, s32[24]{0:T(128)}, u32[]{:S(2)}) copy-start(s32[24]{0:T(128)} %len_hbm.1) | copy-start | bytes 292

commit v5 on v4

--- a/solution.py
+++ b/solution.py
@@ -322,13 +322,12 @@
 
         lax.fori_loop(first + ahead, first + ny, both, 0)
         lax.fori_loop(first + ny - ahead, first + ny, pass_group, 0)
-        if g >= 1:
-            pass_second(g - 1)
         if 2 <= g + 2 <= ring_plus:
             val_point(g + 2)
             norms(g)
     done = min(groups, max(ring_plus - 1, 0))
-    pass_second(groups - 1)
+    for g in range(groups):
+        pass_second(g)
     for g in range(groups - 1):
         end_second(g)
     for k in range(max(groups + 2, 2), ring_plus + 1):

time: 51.4 us -> 50.7 us (0.986); the launches traced: 50.5 us -> 50.6 us
  no operation moved by 1% of the time
where the time goes in v5:
time: 50.7 us; the launch traced here: 50.6 us
  Pallas kernels  48.1 us (95%)
  local copies, waits for them, and re-layouts  1.86 us (4%)
  between operations  0.65 us (1%)
    pallas_call x1, Pallas kernels, shards(): pl.pallas_call(functools.partial(kernel, ny, nx, nz, groups, rank), out_s...  48.1 us

profile of v5, /device:TPU:1, one launch (start us, length us, event | category | flops | bytes accessed | tf_op | source)
XLA Modules:
  0.0 50.6 jit_solution(13330287876487634272)
XLA Ops:
  0.6 0.0 copy-start
  0.6 0.6 %copy-done = s32[24]{0:T(128)S(1)} copy-done((s32[24]{0:T(128)S(1)}, s32[24]{0:T(128)}, u32[]{:S(2)}) %copy-start) | copy-done | bytes 120
  1.3 48.1 %shard_map.68 = f32[2,24,256]{2,1,0:T(8,128)S(1)} custom-call(bf16[24,64,256]{2,1,0:T(8,128)(2,1)} %bitcast.5, bf16[24,256,256]{2,1,0:T(8,128)(2,1)} %og_hbm.1, s32[24]{0:T(128)S(1)} %copy-done, bf16[1024,4096]{1,0:T(8,128)(2,1)} %proj_hbm.1, bf16[256,256]{1,0:T(8,128)(2,1)} %val_hbm.1), custom_call_target="tpu_custom_call" | custom-call | flops 4000000000 | bytes 13000000 | tf_op jit(solution)/shard_map/pallas_call | solution.py:487
  49.4 0.6 %fusion = bf16[24,256]{1,0:T(8,128)(2,1)} fusion(f32[2,24,256]{2,1,0:T(8,128)S(1)} %shard_map.68), kind=kLoop, calls=%fused_computation.2 | loop fusion | bytes 24576 | tf_op jit(solution)/shard_map/convert_element_type | solution.py:500
  50.0 0.6 %slice_bitcast_fusion = f32[24,256]{1,0:T(8,128)} fusion(f32[2,24,256]{2,1,0:T(8,128)S(1)} %shard_map.68), kind=kLoop, calls=%fused_computation.1 | loop fusion | bytes 49152 | tf_op jit(solution)/shard_map/squeeze | solution.py:500
Async XLA Ops:
  0.6 0.7 %copy-start = (s32[24]{0:T(128)S(1)}, s32[24]{0:T(128)}, u32[]{:S(2)}) copy-start(s32[24]{0:T(128)} %len_hbm.1) | copy-start | bytes 292

commit v6 on v5

--- a/solution.py
+++ b/solution.py
@@ -60,7 +60,7 @@
     for o in range(1, ex_n):
         greet(plane(o // nx, o % nx), par)
 
-    for o in range(1, nz):
+    for o in sorted({1, nz - 1}):
         greet(ex, depth(o) * 2 + core)
     greet(ex, z * 2 + 1 - core)
 
@@ -155,7 +155,7 @@
         lax.fori_loop(0, ex_n, pack, 0, unroll=4)
         recv_a[g, ex] = send_a[g, ex]
         if g == 0:
-            pl.semaphore_wait(barrier, ex_n - 1 + nz - 1 + 1)
+            pl.semaphore_wait(barrier, ex_n - 1 + len({1, nz - 1}) + 1)
 
         for o in range(1, ex_n):
             a2a(g, o).start()

time: 50.7 us -> 50.6 us (level)
  no operation moved by 1% of the time
where the time goes in v6:
time: 50.6 us; the launch traced here: 50.2 us
  Pallas kernels  47.7 us (94%)
  local copies, waits for them, and re-layouts  1.86 us (4%)
  between operations  0.65 us (1%)
    pallas_call x1, Pallas kernels, shards(): pl.pallas_call(functools.partial(kernel, ny, nx, nz, groups, rank), out_s...  47.7 us

profile of v6, /device:TPU:1, one launch (start us, length us, event | category | flops | bytes accessed | tf_op | source)
XLA Modules:
  0.0 50.2 jit_solution(12219737115861597046)
XLA Ops:
  0.6 0.0 copy-start
  0.6 0.6 %copy-done = s32[24]{0:T(128)S(1)} copy-done((s32[24]{0:T(128)S(1)}, s32[24]{0:T(128)}, u32[]{:S(2)}) %copy-start) | copy-done | bytes 120
  1.3 47.7 %shard_map.68 = f32[2,24,256]{2,1,0:T(8,128)S(1)} custom-call(bf16[24,64,256]{2,1,0:T(8,128)(2,1)} %bitcast.5, bf16[24,256,256]{2,1,0:T(8,128)(2,1)} %og_hbm.1, s32[24]{0:T(128)S(1)} %copy-done, bf16[1024,4096]{1,0:T(8,128)(2,1)} %proj_hbm.1, bf16[256,256]{1,0:T(8,128)(2,1)} %val_hbm.1), custom_call_target="tpu_custom_call" | custom-call | flops 4000000000 | bytes 13000000 | tf_op jit(solution)/shard_map/pallas_call | solution.py:487
  49.0 0.6 %fusion = bf16[24,256]{1,0:T(8,128)(2,1)} fusion(f32[2,24,256]{2,1,0:T(8,128)S(1)} %shard_map.68), kind=kLoop, calls=%fused_computation.2 | loop fusion | bytes 24576 | tf_op jit(solution)/shard_map/convert_element_type | solution.py:500
  49.6 0.6 %slice_bitcast_fusion = f32[24,256]{1,0:T(8,128)} fusion(f32[2,24,256]{2,1,0:T(8,128)S(1)} %shard_map.68), kind=kLoop, calls=%fused_computation.1 | loop fusion | bytes 49152 | tf_op jit(solution)/shard_map/squeeze | solution.py:500
Async XLA Ops:
  0.6 0.7 %copy-start = (s32[24]{0:T(128)S(1)}, s32[24]{0:T(128)}, u32[]{:S(2)}) copy-start(s32[24]{0:T(128)} %len_hbm.1) | copy-start | bytes 292
